TPU v7x, 32 devices: a whole 2x2x4 slice. The times are simulated.
32 devices in a mesh: dp: 4 (over y, x), vocab: 8 (over z, core).
Axes of the slice: x: 2, y: 2, z: 4, core: 2. Of those that a mesh axis runs over, the one named last changes fastest.
Arguments:
- hidden: bfloat16 [128, 3584], P(('dp', 'vocab')), may hold values from -6 to 6
- head_weight: bfloat16 [3584, 256000], P(None, ('dp', 'vocab')), may hold values from -0.75 to 0.75
- teacher_ids: int32 [128, 128], P(('dp', 'vocab')), may hold values from 0 to 255999
- teacher_probs: float32 [128, 128], P(('dp', 'vocab')), may hold values from 0.0001 to 0.015
- target_ids: int32 [128], P(('dp', 'vocab')), may hold values from 0 to 255999
Outputs:
- token_loss: float32 [128], P(('dp', 'vocab'))
- hidden_grad: bfloat16 [128, 3584], P(('dp', 'vocab'))
All inputs are finite; a program needn't handle non-finite values.
Results may differ from a plain program's by a relative error of at most 0.004.
Values may be sent and summed in bfloat16 or wider, within the bound.
A program may use at most 128 MiB of HBM per device.

v0:
```python
import functools
import jax
import jax.numpy as jnp
from jax import lax
from jax.experimental import pallas as pl
from jax.experimental.pallas import tpu as pltpu
from jax.sharding import PartitionSpec as P

SOFT_CAP = 30.0
CE_WEIGHT = 0.5
LOSS_SCALE = 8.0
BLOCK = 1024
LANES = 128
ROW_CHUNK = 512
AXES = ("dp", "vocab")
MESH = pl.DeviceIdType.MESH
NT = (((1,), (1,)), ((), ()))


def head_kernel(width, hidden_ref, w_ref, ids_ref, hi_probs_ref, lo_probs_ref, targets_ref,
                acc_ref, stats_ref, sparse_ref):
    step = pl.program_id(0)
    steps = pl.num_programs(0)
    tokens, depth = hidden_ref.shape
    kept = ids_ref.shape[1]
    groups = sparse_ref.shape[0]
    group_rows = 16 * pl.cdiv(groups, 16)

    @pl.when(step == 0)
    def _():
        acc_ref[...] = jnp.zeros_like(acc_ref)
        stats_ref[...] = jnp.zeros_like(stats_ref)
        group_row = lax.broadcasted_iota(jnp.int32, (group_rows, kept), 0)
        lane_row = lax.broadcasted_iota(jnp.int32, (LANES, kept), 0)

        def one_token(t, carry):
            ids = ids_ref[pl.ds(t, 1), :]
            high = jnp.where(group_row == (ids >> 7), 1.0, 0.0).astype(jnp.bfloat16)
            same = lane_row == (ids & 127)
            first = jnp.where(same, hi_probs_ref[pl.ds(t, 1), :], 0.0).astype(jnp.bfloat16)
            second = jnp.where(same, lo_probs_ref[pl.ds(t, 1), :], 0.0).astype(jnp.bfloat16)
            rows = lax.dot_general(
                jnp.concatenate([high, high], axis=1),
                jnp.concatenate([first, second], axis=1),
                NT, preferred_element_type=jnp.float32)
            sparse_ref[:, pl.ds(t, 1), :] = rows[:groups].reshape(groups, 1, LANES)
            return carry

        lax.fori_loop(0, tokens, one_token, 0, unroll=8)

    def block(columns):
        w = w_ref.at[pl.ds(0, columns)]
        logits = lax.dot_general(hidden_ref[...], w[...], NT, preferred_element_type=jnp.float32)
        ratio = jnp.tanh(logits * (1.0 / SOFT_CAP))
        capped = SOFT_CAP * ratio
        slope = 1.0 - ratio * ratio
        lane = lax.broadcasted_iota(jnp.int32, (tokens, columns), 1)
        exps = jnp.exp(capped)
        sparse = jnp.concatenate(
            [sparse_ref[step * (BLOCK // LANES) + i] for i in range(pl.cdiv(columns, LANES))],
            axis=1)[:, :columns]
        sparse = sparse + jnp.where(lane + step * BLOCK == targets_ref[...], CE_WEIGHT, 0.0)
        stats_ref[:, 0:1] += jnp.sum(exps, axis=1, keepdims=True)
        stats_ref[:, 1:2] += jnp.sum(capped * sparse, axis=1, keepdims=True)
        grads = jnp.concatenate([exps * slope, sparse * slope], axis=0).astype(jnp.bfloat16)
        for start in range(0, depth, ROW_CHUNK):
            part = slice(start, start + ROW_CHUNK)
            acc_ref[:, part] += jnp.dot(grads, w[:, part], preferred_element_type=jnp.float32)

    last = width - (pl.cdiv(width, BLOCK) - 1) * BLOCK

    @pl.when(step < steps - 1)
    def _():
        block(BLOCK)

    @pl.when(step == steps - 1)
    def _():
        block(last)


def head_pass(hidden, head_weight, local_ids, probs, local_targets):
    tokens, depth = hidden.shape
    width = head_weight.shape[1]
    kept = local_ids.shape[1]
    groups = pl.cdiv(width, LANES)
    hi_probs = probs.astype(jnp.bfloat16).astype(jnp.float32)
    lo_probs = probs - hi_probs
    full = lambda shape: pl.BlockSpec(shape, lambda j: (0, 0), pipeline_mode=pl.Buffered(1))
    return pl.pallas_call(
        functools.partial(head_kernel, width),
        grid=(pl.cdiv(width, BLOCK),),
        in_specs=[
            full((tokens, depth)),
            pl.BlockSpec((BLOCK, depth), lambda j: (j, 0)),
            full((tokens, kept)),
            full((tokens, kept)),
            full((tokens, kept)),
            full((tokens, 1)),
        ],
        out_specs=[full((2 * tokens, depth)), full((tokens, LANES))],
        out_shape=[
            jax.ShapeDtypeStruct((2 * tokens, depth), jnp.float32),
            jax.ShapeDtypeStruct((tokens, LANES), jnp.float32),
        ],
        scratch_shapes=[pltpu.VMEM((groups, tokens, LANES), jnp.float32)],
        compiler_params=pltpu.CompilerParams(vmem_limit_bytes=58 * 1024 * 1024),
        cost_estimate=pl.CostEstimate(
            flops=6 * tokens * depth * width, bytes_accessed=2 * depth * width,
            transcendentals=2 * tokens * width),
        name="head_pass",
    )(hidden, head_weight.T, local_ids, hi_probs, lo_probs, local_targets[:, None])


def meet(nd, nv):
    d, v = lax.axis_index("dp"), lax.axis_index("vocab")
    barrier = pltpu.get_barrier_semaphore()
    peers_v = [(d, lax.rem(v + o, nv)) for o in range(1, nv)]
    peers_d = [(lax.rem(d + o, nd), v) for o in range(1, nd)]
    for peer in peers_v + peers_d:
        pl.semaphore_signal(barrier, inc=1, device_id=peer, device_id_type=MESH)
    pl.semaphore_wait(barrier, nv + nd - 2)
    return d, v, peers_d, peers_v


def remote(src, dst, send, recv, peer):
    return pltpu.make_async_remote_copy(
        src_ref=src, dst_ref=dst, send_sem=send, recv_sem=recv,
        device_id=peer, device_id_type=MESH)


def gather_kernel(nd, nv, *refs):
    ins, outs = refs[:3], refs[3:6]
    send_v, recv_v, send_d, recv_d = refs[6:]
    d, v, peers_d, peers_v = meet(nd, nv)
    for i in range(3):
        outs[i][d * nv + v] = ins[i][...]
    copies = []
    for o, peer in enumerate(peers_v):
        for i in range(3):
            copy = remote(ins[i], outs[i].at[d * nv + v], send_v.at[i, o], recv_v.at[i, v], peer)
            copy.start()
            copies.append(copy)
    for o, peer in enumerate(peers_v):
        for i in range(3):
            source = peer[1]
            remote(ins[i], outs[i].at[d * nv + source], send_v.at[i, o],
                   recv_v.at[i, source], peer).wait_recv()
    for o, peer in enumerate(peers_d):
        for i in range(3):
            rows = outs[i].at[pl.ds(d * nv, nv)]
            copy = remote(rows, rows, send_d.at[i, o], recv_d.at[i, d], peer)
            copy.start()
            copies.append(copy)
    for o, peer in enumerate(peers_d):
        for i in range(3):
            rows = outs[i].at[pl.ds(peer[0] * nv, nv)]
            remote(rows, rows, send_d.at[i, o], recv_d.at[i, peer[0]], peer).wait_recv()
    for copy in copies:
        copy.wait_send()


def totals_kernel(nd, nv, in_ref, out_ref, slots_v, slots_d, held, send_v, recv_v, send_d, recv_d):
    d, v, peers_d, peers_v = meet(nd, nv)
    copies = []
    for peers, me, src, slots, send, recv, axis, result in (
        (peers_v, v, in_ref, slots_v, send_v, recv_v, 1, held),
        (peers_d, d, held, slots_d, send_d, recv_d, 0, out_ref),
    ):
        for o, peer in enumerate(peers):
            copy = remote(src, slots.at[me], send.at[o], recv.at[me], peer)
            copy.start()
            copies.append(copy)
        slots[me] = src[...]
        for o, peer in enumerate(peers):
            source = peer[axis]
            remote(src, slots.at[source], send.at[o], recv.at[source], peer).wait_recv()
        result[...] = jnp.sum(slots[...], axis=0)
    for copy in copies:
        copy.wait_send()


def reduce_kernel(nd, nv, in_ref, out_ref, slots_d, slots_v, held, send_d, recv_d, send_v, recv_v):
    d, v, peers_d, peers_v = meet(nd, nv)
    copies = []
    for o, peer in enumerate(peers_d):
        copy = remote(in_ref.at[peer[0]], slots_d.at[d], send_d.at[o], recv_d.at[d], peer)
        copy.start()
        copies.append(copy)
    held[...] = in_ref[d].astype(jnp.float32)
    for o, peer in enumerate(peers_d):
        source = peer[0]
        remote(in_ref.at[d], slots_d.at[source], send_d.at[o], recv_d.at[source], peer).wait_recv()
        held[...] += slots_d[source].astype(jnp.float32)
    for o, peer in enumerate(peers_v):
        copy = remote(held.at[peer[1]], slots_v.at[v], send_v.at[o], recv_v.at[v], peer)
        copy.start()
        copies.append(copy)
    total = held[v]
    for o, peer in enumerate(peers_v):
        source = peer[1]
        remote(held.at[v], slots_v.at[source], send_v.at[o], recv_v.at[source], peer).wait_recv()
        total = total + slots_v[source]
    out_ref[...] = total.astype(out_ref.dtype)
    for copy in copies:
        copy.wait_send()


def comm_call(kernel, number, name, args, out_shape, scratch):
    vmem = pl.BlockSpec(memory_space=pltpu.VMEM)
    return pl.pallas_call(
        kernel,
        out_shape=out_shape,
        in_specs=[vmem] * len(args),
        out_specs=[vmem] * len(out_shape),
        scratch_shapes=scratch,
        compiler_params=pltpu.CompilerParams(
            collective_id=number, has_side_effects=True, vmem_limit_bytes=48 * 1024 * 1024),
        name=name,
    )(*args)


def per_device(nd, nv, hidden, head_weight, teacher_ids, teacher_probs, target_ids):
    width = head_weight.shape[1]
    local_tokens, kept = teacher_ids.shape
    depth = hidden.shape[1]
    count = nd * nv
    tokens = count * local_tokens
    position = lax.axis_index(AXES)
    sems = lambda *shape: pltpu.SemaphoreType.DMA(shape)
    rows = local_tokens * depth // LANES
    pad = 8 * pl.cdiv(local_tokens + 1, 8)
    target_row = jnp.pad(target_ids, (0, kept - local_tokens))[None, :]
    ids = jnp.pad(jnp.concatenate([teacher_ids, target_row], axis=0),
                  ((0, pad - local_tokens - 1), (0, 0)))
    probs = jnp.pad(teacher_probs, ((0, pad - local_tokens), (0, 0)))
    args = (hidden.reshape(rows, LANES), ids, probs)
    got = comm_call(
        functools.partial(gather_kernel, nd, nv), 0, "gather_inputs", args,
        [jax.ShapeDtypeStruct((count,) + a.shape, a.dtype) for a in args],
        [sems(3, nv), sems(3, nv), sems(3, nd), sems(3, nd)])
    all_hidden = got[0].reshape(tokens, depth)
    local = got[1] - position * width
    local_ids = local[:, :local_tokens].reshape(tokens, kept)
    local_targets = local[:, local_tokens, :local_tokens].reshape(tokens)
    all_probs = got[2][:, :local_tokens].reshape(tokens, kept)
    acc, stats = head_pass(all_hidden, head_weight, local_ids, all_probs, local_targets)
    block = (8, tokens)
    totals = comm_call(
        functools.partial(totals_kernel, nd, nv), 1, "sum_stats", (stats[:, :8].T,),
        [jax.ShapeDtypeStruct(block, jnp.float32)],
        [pltpu.VMEM((nv,) + block, jnp.float32), pltpu.VMEM((nd,) + block, jnp.float32),
         pltpu.VMEM(block, jnp.float32), sems(nv), sems(nv), sems(nd), sems(nd)])[0]
    exp_sum, dots = totals[0], totals[1]
    teacher_sum = jnp.sum(all_probs, axis=1)
    scale = LOSS_SCALE * (teacher_sum + CE_WEIGHT) / exp_sum
    part = (scale[:, None] * acc[:tokens] - LOSS_SCALE * acc[tokens:]).astype(jnp.bfloat16)
    piece = (rows, LANES)
    grad = comm_call(
        functools.partial(reduce_kernel, nd, nv), 2, "sum_grads",
        (part.reshape((nd, nv) + piece),),
        [jax.ShapeDtypeStruct(piece, jnp.bfloat16)],
        [pltpu.VMEM((nd, nv) + piece, jnp.bfloat16), pltpu.VMEM((nv,) + piece, jnp.float32),
         pltpu.VMEM((nv,) + piece, jnp.float32), sems(nd), sems(nd), sems(nv), sems(nv)])[0]
    own = lambda x: lax.dynamic_slice_in_dim(x, position * local_tokens, local_tokens)
    own_sum = jnp.sum(teacher_probs, axis=1)
    loss = (
        jnp.sum(teacher_probs * jnp.log(teacher_probs), axis=1)
        - own(dots)
        + (own_sum + CE_WEIGHT) * jnp.log(own(exp_sum))
    )
    return loss, grad.reshape(local_tokens, depth)


def solution(mesh):
    in_specs = (
        P(AXES, None),
        P(None, AXES),
        P(AXES, None),
        P(AXES, None),
        P(AXES),
    )
    out_specs = (P(AXES), P(AXES, None))
    return jax.shard_map(
        functools.partial(per_device, mesh.shape["dp"], mesh.shape["vocab"]),
        mesh=mesh, in_specs=in_specs, out_specs=out_specs, check_vma=False
    )
```

profile of v0, /device:TPU:0, one launch (start us, length us, event | category | flops | bytes accessed | tf_op | source)
XLA Modules:
  0.0 122.4 jit_solution(7913495770868065056)
XLA Ops:
  0.6 0.7 pad_bitcast_fusion
  1.3 0.8 fusion.3
  2.1 0.7 pad_add_fusion
  2.8 0.7 pad.14.refs_2_
  3.5 0.8 reshape.42.refs_0_
  4.3 26.9 %gather_inputs.1 = (bf16[32,112,128]{2,1,0:T(8,128)(2,1)S(1)}, s32[32,8,128]{2,1,0:T(8,128)S(1)}, f32[32,8,128]{2,1,0:T(8,128)S(1)}) custom-call(bf16[112,128]{1,0:T(8,128)(2,1)S(1)} %reshape.42.refs_0_, s32[8,128]{1,0:T(8,128)S(1)} %pad.13.refs_1_, f32[8,128]{1,0:T(8,128)S(1)} %pad.14.refs_2_), custom_call_target="tpu_custom_call" | custom-call | tf_op jit(solution)/shard_map/gather_inputs/pallas_call | solution.py:210
  31.2 1.9 %reshape.43.hidden_ref = bf16[128,3584]{1,0:T(8,128)(2,1)} reshape(bf16[32,112,128]{2,1,0:T(8,128)(2,1)S(1)} %get-tuple-element.7) | data formatting | bytes 1835008 | tf_op jit(solution)/shard_map/reshape | solution.py:241
  33.1 0.1 slice_reduce_fusion.1
  33.3 0.1 mul.50
  33.4 0.7 fusion
  34.0 0.1 slice_reduce_fusion
  34.1 0.6 slice.32
  34.7 0.7 broadcast_in_dim_reshape_squeeze.4.targets_ref
  35.4 47.1 %head_pass.1 = (f32[256,3584]{1,0:T(8,128)}, f32[128,128]{1,0:T(8,128)}) custom-call(bf16[128,3584]{1,0:T(8,128)(2,1)} %reshape.43.hidden_ref, bf16[8000,3584]{1,0:T(8,128)(2,1)} %bitcast.19, s32[128,128]{1,0:T(8,128)} %bitcast.18, f32[128,128]{1,0:T(8,128)} %get-tuple-element.17.hi_probs_ref, f32[128,128]{1,0:T(8,128)} %get-tuple-element.16.lo_probs_ref, ...), custom_call_target="tpu_custom_call" | custom-call | flops 22020096000 | bytes 57344000 | tf_op jit(solution)/shard_map/head_pass/pallas_call | solution.py:89
  82.6 0.9 copy.10
  83.5 10.6 %sum_stats.1 = f32[8,128]{1,0:T(8,128)S(1)} custom-call(f32[8,128]{1,0:T(8,128)S(1)} %slice_bitcast_fusion.in_ref), custom_call_target="tpu_custom_call" | custom-call | tf_op jit(solution)/shard_map/sum_stats/pallas_call | solution.py:210
  94.1 2.4 %subtract_convert_fusion = bf16[128,3584]{1,0:T(8,128)(2,1)S(1)} fusion(f32[256,3584]{1,0:T(8,128)} %get-tuple-element.11, f32[128]{0:T(128)S(1)} %bitcast_divide_fusion), kind=kLoop, calls=%fused_computation | loop fusion | flops 1835008 | bytes 4588032 | tf_op jit(solution)/shard_map/convert_element_type | solution.py:256
  96.5 0.6 fusion.2
  97.1 1.1 reshape.46.in_ref
  98.2 23.5 %sum_grads.1 = bf16[112,128]{1,0:T(8,128)(2,1)S(1)} custom-call(bf16[4,8,112,128]{3,2,1,0:T(8,128)(2,1)S(1)} %reshape.46.in_ref), custom_call_target="tpu_custom_call" | custom-call | tf_op jit(solution)/shard_map/sum_grads/pallas_call | solution.py:210
  121.8 0.6 reshape.47
  (6 shorter events, 0.0 us)
where the time goes:
time: 123 us; the launch traced here: 122 us
  Pallas kernels  108 us (88%)
  local copies, waits for them, and re-layouts  8.24 us (7%)
  other arithmetic  5.27 us (4%)
    pallas_call x3, Pallas kernels, comm_call(): pl.pallas_call(kernel, out_shape=out_shape, in_specs=[vmem] * len(args),...  61 us
    pallas_call x1, Pallas kernels, head_pass(): pl.pallas_call(functools.partial(head_kernel, width), grid=(pl.cdiv(width...  47.1 us

commit v1 on v0

v1 whole, which is shorter than its diff:
```python
import functools
import jax
import jax.numpy as jnp
from jax import lax
from jax.experimental import pallas as pl
from jax.experimental.pallas import tpu as pltpu
from jax.sharding import PartitionSpec as P

SOFT_CAP = 30.0
CE_WEIGHT = 0.5
LOSS_SCALE = 8.0
BLOCK = 640
CHUNK = 512
LANES = 128
PACK = 16
AXES = ("dp", "vocab")
MESH = pl.DeviceIdType.MESH
NT = (((1,), (1,)), ((), ()))


def remote(src, dst, send, recv, peer):
    return pltpu.make_async_remote_copy(
        src_ref=src, dst_ref=dst, send_sem=send, recv_sem=recv,
        device_id=peer, device_id_type=MESH)


def fused_kernel(nd, nv, hid_in, ids_in, probs_in, targets_in, w_hbm, loss_ref, grad_ref,
                 w_ref, hid, near, near32, small, cells, grads, probs, exp_part, dot_part,
                 column, totals, slots_v, slots_d, own1, send1, send2, own2, send3, recv3,
                 w_sem, zs_send, zs_recv, zh_send, zh_recv, ds_send, ds_recv, dh_send, dh_recv,
                 cs_send, cs_recv, ch_send, ch_recv, tv_send, tv_recv, td_send, td_recv,
                 r1_send, r1_recv, r2_send, r2_recv, r3_send, r3_recv):
    local_tokens, depth = hid_in.shape
    tokens = hid.shape[0]
    width = w_ref.shape[0]
    kept = ids_in.shape[1]
    nz = nv // 2
    rows = nz * local_tokens
    half = nd * rows
    chunks = depth // CHUNK
    d, v = lax.axis_index("dp"), lax.axis_index("vocab")
    z, k = v // 2, lax.rem(v, 2)
    mine = d * 2 + k
    zs = [lax.rem(z + o, nz) for o in range(1, nz)]
    dps = [lax.rem(d + o, nd) for o in range(1, nd)]
    sibling = (d, z * 2 + 1 - k)
    z_peer = lambda q: (d, q * 2 + k)
    d_peer = lambda q: (q, v)

    full_blocks, tail = width // BLOCK, width % BLOCK
    pieces = full_blocks + (tail > 0)

    def w_copy(j, size):
        at = pl.ds(pl.multiple_of(j * BLOCK, BLOCK), size)
        return pltpu.make_async_copy(w_hbm.at[at], w_ref.at[at], w_sem.at[j])

    def start_w(j, carry):
        w_copy(j, BLOCK).start()
        return carry

    lax.fori_loop(0, full_blocks, start_w, 0)
    if tail:
        w_copy(full_blocks, tail).start()

    own_block = mine * nz + z
    for i in range(local_tokens):
        small[own_block, 2 * local_tokens + i:2 * local_tokens + i + 1, :] = jnp.full(
            (1, kept), targets_in[i], jnp.int32).astype(jnp.float32)
    small[own_block, 0:local_tokens, :] = ids_in[...].astype(jnp.float32)
    small[own_block, local_tokens:2 * local_tokens, :] = probs_in[...]
    near[z] = hid_in[...]

    barrier = pltpu.get_barrier_semaphore()
    peers_v = [(d, lax.rem(v + o, nv)) for o in range(1, nv)]
    peers_d = [d_peer(q) for q in dps]
    for peer in peers_v + peers_d:
        pl.semaphore_signal(barrier, inc=1, device_id=peer, device_id_type=MESH)
    pl.semaphore_wait(barrier, nv + nd - 2)

    sent = []

    def go(copy):
        copy.start()
        sent.append(copy)

    for o, q in enumerate(zs):
        go(remote(small.at[own_block], small.at[own_block], zs_send.at[o], zs_recv.at[z],
                  z_peer(q)))
    for o, q in enumerate(zs):
        go(remote(hid_in, near.at[z], zh_send.at[o], zh_recv.at[z], z_peer(q)))
    for o, q in enumerate(zs):
        at = small.at[mine * nz + q]
        remote(at, at, zs_send.at[o], zs_recv.at[q], z_peer(q)).wait_recv()

    def small_at(group):
        return small.at[pl.ds(group * nz, nz)]

    def hid_at(group):
        return hid.at[pl.ds(pl.multiple_of(group * rows, rows), rows)]

    at = small_at(mine)
    for o, q in enumerate(dps):
        go(remote(at, at, ds_send.at[o], ds_recv.at[d], d_peer(q)))
    go(remote(at, at, cs_send.at[d], cs_recv.at[d], sibling))

    for o, q in enumerate(zs):
        remote(hid_in, near.at[q], zh_send.at[o], zh_recv.at[q], z_peer(q)).wait_recv()
    for q in range(nz):
        near32[q * local_tokens:(q + 1) * local_tokens, :] = near[q].astype(jnp.float32)
    hid[pl.ds(pl.multiple_of(mine * rows, rows), rows), :] = near32[...].astype(jnp.bfloat16)
    at = hid_at(mine)
    for o, q in enumerate(dps):
        go(remote(at, at, dh_send.at[o], dh_recv.at[d], d_peer(q)))
    go(remote(at, at, ch_send.at[d], ch_recv.at[d], sibling))

    for o, q in enumerate(dps):
        at = small_at(q * 2 + k)
        remote(at, at, ds_send.at[o], ds_recv.at[q], d_peer(q)).wait_recv()
        go(remote(at, at, cs_send.at[q], cs_recv.at[q], sibling))
    for q in range(nd):
        at = small_at(q * 2 + 1 - k)
        remote(at, at, cs_send.at[q], cs_recv.at[q], sibling).wait_recv()

    groups = pl.cdiv(width, LANES)
    group_rows = 16 * pl.cdiv(groups, 16)
    offset = (d * nv + v) * width
    group_row = lax.broadcasted_iota(jnp.int32, (group_rows, kept), 0)
    lane_row = lax.broadcasted_iota(jnp.int32, (LANES, kept), 0)
    flat = group_row * LANES + lax.broadcasted_iota(jnp.int32, (group_rows, LANES), 1)
    per_step = 8 // local_tokens

    def scatter(step, carry):
        first = pl.multiple_of(step * 8, 8)
        found = []
        for i in range(8):
            block = step * per_step + i // local_tokens
            r = i % local_tokens
            ids = small[block, r:r + 1, :].astype(jnp.int32) - offset
            p = small[block, local_tokens + r:local_tokens + r + 1, :]
            target = small[block, 2 * local_tokens + r:2 * local_tokens + r + 1, :]
            target = target.astype(jnp.int32) - offset
            probs[pl.ds(first + i, 1), :] = p
            high = p.astype(jnp.bfloat16).astype(jnp.float32)
            inside = group_row == (ids >> 7)
            left = jnp.concatenate(
                [jnp.where(inside, high, 0.0), jnp.where(inside, p - high, 0.0)],
                axis=0).astype(jnp.bfloat16)
            right = jnp.where(lane_row == (ids & 127), 1.0, 0.0).astype(jnp.bfloat16)
            both = lax.dot_general(left, right, NT, preferred_element_type=jnp.float32)
            found.append(both[:group_rows] + both[group_rows:]
                         + jnp.where(flat == target, CE_WEIGHT, 0.0))
        cells[:, pl.ds(first, 8), :] = jnp.swapaxes(jnp.stack(found, axis=0), 0, 1)[:groups]
        return carry

    lax.fori_loop(0, tokens // 16, scatter, 0)
    for o, q in enumerate(dps):
        at = hid_at(q * 2 + k)
        remote(at, at, dh_send.at[o], dh_recv.at[q], d_peer(q)).wait_recv()
        go(remote(at, at, ch_send.at[q], ch_recv.at[q], sibling))
    lax.fori_loop(tokens // 16, tokens // 8, scatter, 0)
    for q in range(nd):
        at = hid_at(q * 2 + 1 - k)
        remote(at, at, ch_send.at[q], ch_recv.at[q], sibling).wait_recv()
    for copy in sent:
        copy.wait_send()
    sent.clear()

    exp_part[...] = jnp.zeros_like(exp_part)
    dot_part[...] = jnp.zeros_like(dot_part)

    def block(j, size):
        w_copy(j, size).wait()
        w = w_ref[pl.ds(pl.multiple_of(j * BLOCK, BLOCK), size), :]
        logits = lax.dot_general(w, hid[...], NT, preferred_element_type=jnp.float32).T
        for i in range(pl.cdiv(size, LANES)):
            n = min(LANES, size - i * LANES)
            group = j * (BLOCK // LANES) + i
            ratio = jnp.tanh(logits[:, i * LANES:i * LANES + n] * (1.0 / SOFT_CAP))
            capped = SOFT_CAP * ratio
            slope = 1.0 - ratio * ratio
            exps = jnp.exp(capped)
            sparse = cells[group, :, 0:n]
            cells[group, :, 0:n] = exps * slope
            grads[:, pl.ds(pl.multiple_of(group * LANES, LANES), n)] = (
                sparse * slope).astype(jnp.bfloat16)
            exp_part[:, 0:n] += exps
            dot_part[:, 0:n] += capped * sparse

    def full_block(j, carry):
        block(j, BLOCK)
        return carry

    lax.fori_loop(0, full_blocks, full_block, 0)
    if tail:
        block(full_blocks, tail)

    totals[...] = jnp.zeros_like(totals)
    totals[0:1, :] = jnp.sum(exp_part[...].T, axis=0, keepdims=True)
    totals[1:2, :] = jnp.sum(dot_part[...].T, axis=0, keepdims=True)
    for peers, me, slots, send, recv, axis in (
        (peers_v, v, slots_v, tv_send, tv_recv, 1),
        (peers_d, d, slots_d, td_send, td_recv, 0),
    ):
        slots[me] = totals[...]
        for o, peer in enumerate(peers):
            go(remote(slots.at[me], slots.at[me], send.at[o], recv.at[me], peer))
        for o, peer in enumerate(peers):
            at = slots.at[peer[axis]]
            remote(at, at, send.at[o], recv.at[peer[axis]], peer).wait_recv()
        totals[...] = jnp.sum(slots[...], axis=0)
    for copy in sent:
        copy.wait_send()
    sent.clear()

    spread = lambda row: jnp.broadcast_to(row, (LANES, tokens)).T
    exp_sum = spread(totals[0:1, :])
    exp_part[...] = exp_sum
    dot_part[...] = spread(totals[1:2, :])
    teacher_sum = jnp.sum(probs[...], axis=1, keepdims=True)
    column[...] = LOSS_SCALE * (teacher_sum + CE_WEIGHT) / exp_sum

    own_row = mine * rows + z * local_tokens
    for i in range(local_tokens):
        p = probs_in[i:i + 1, :]
        loss_ref[i:i + 1, :] = (
            jnp.sum(p * jnp.log(p), axis=1, keepdims=True)
            - dot_part[pl.ds(own_row + i, 1), :]
            + (jnp.sum(p, axis=1, keepdims=True) + CE_WEIGHT)
            * jnp.log(exp_part[pl.ds(own_row + i, 1), :]))

    def scale_group(group, n):
        at = pl.ds(pl.multiple_of(group * LANES, LANES), n)
        grads[:, at] = (column[:, 0:n] * cells[group, :, 0:n]
                        - LOSS_SCALE * grads[:, at].astype(jnp.float32)).astype(jnp.bfloat16)

    def scale_full(group, carry):
        scale_group(group, LANES)
        return carry

    lax.fori_loop(0, width // LANES, scale_full, 0)
    if width % LANES:
        scale_group(width // LANES, width % LANES)

    def cols(c):
        return pl.ds(pl.multiple_of(c * CHUNK, CHUNK), CHUNK)

    def copy1(c):
        return remote(send1.at[lax.rem(c, 2)], hid.at[pl.ds(0, half), cols(c)],
                      r1_send.at[c], r1_recv.at[c], sibling)

    def copy2(c, o, q, source):
        return remote(send2.at[lax.rem(c, 2), pl.ds(pl.multiple_of(q * rows, rows), rows)],
                      hid.at[pl.ds(pl.multiple_of(half + source * rows, rows), rows), cols(c)],
                      r2_send.at[c, o], r2_recv.at[c, source], d_peer(q))

    def copy3(c, o, q, source):
        return remote(send3.at[lax.rem(c, 2), q], recv3.at[c, source],
                      r3_send.at[c, o], r3_recv.at[c, source], z_peer(q))

    def grad_step(c, carry):
        @pl.when(c < chunks)
        def _():
            acc = jnp.dot(grads[...], w_ref[:, cols(c)], preferred_element_type=jnp.float32)
            acc = acc.reshape(nd, 2, rows, CHUNK)
            slot = lax.rem(c, 2)
            own1[slot] = jnp.where(k == 0, acc[:, 0], acc[:, 1]).reshape(half, CHUNK)
            send1[slot] = jnp.where(k == 0, acc[:, 1], acc[:, 0]).reshape(half, CHUNK).astype(
                jnp.bfloat16)
            copy1(c).start()

        @pl.when((c >= 1) & (c < chunks + 1))
        def _():
            b = c - 1
            slot = lax.rem(b, 2)
            copy1(b).wait()
            total = own1[slot] + hid[0:half, cols(b)].astype(jnp.float32)
            own1[slot] = total
            send2[slot] = total.astype(jnp.bfloat16)
            for o, q in enumerate(dps):
                copy2(b, o, q, d).start()
            own2[slot] = own1[slot, pl.ds(pl.multiple_of(d * rows, rows), rows), :]

        @pl.when((c >= 2) & (c < chunks + 2))
        def _():
            b = c - 2
            slot = lax.rem(b, 2)
            total = own2[slot]
            for o, q in enumerate(dps):
                copy2(b, o, q, q).wait_recv()
                at = pl.ds(pl.multiple_of(half + q * rows, rows), rows)
                total = total + hid[at, cols(b)].astype(jnp.float32)
            for o, q in enumerate(dps):
                copy2(b, o, q, d).wait_send()
            for q in range(nz):
                send3[slot, q] = total[q * local_tokens:(q + 1) * local_tokens]
            for o, q in enumerate(zs):
                copy3(b, o, q, z).start()
            recv3[b, z] = send3[slot, z]

        @pl.when(c >= 3)
        def _():
            b = c - 3
            for o, q in enumerate(zs):
                copy3(b, o, q, q).wait_recv()
            for o, q in enumerate(zs):
                copy3(b, o, q, z).wait_send()
            total = recv3[b, 0]
            for q in range(1, nz):
                total = total + recv3[b, q]
            grad_ref[:, cols(b)] = total.astype(jnp.bfloat16)

        return carry

    lax.fori_loop(0, chunks + 3, grad_step, 0)


def per_device(nd, nv, hidden, head_weight, teacher_ids, teacher_probs, target_ids):
    local_tokens, depth = hidden.shape
    width = head_weight.shape[1]
    kept = teacher_ids.shape[1]
    count = nd * nv
    tokens = count * local_tokens
    nz = nv // 2
    rows = nz * local_tokens
    half = nd * rows
    chunks = depth // CHUNK
    groups = pl.cdiv(width, LANES)
    f32, bf16 = jnp.float32, jnp.bfloat16
    sems = lambda *shape: pltpu.SemaphoreType.DMA(shape)
    vmem = pl.BlockSpec(memory_space=pltpu.VMEM)
    loss, grad = pl.pallas_call(
        functools.partial(fused_kernel, nd, nv),
        in_specs=[vmem, vmem, vmem, pl.BlockSpec(memory_space=pltpu.SMEM),
                  pl.BlockSpec(memory_space=pl.ANY)],
        out_specs=[vmem, vmem],
        out_shape=[jax.ShapeDtypeStruct((local_tokens, LANES), f32),
                   jax.ShapeDtypeStruct((local_tokens, depth), bf16)],
        scratch_shapes=[
            pltpu.VMEM((width, depth), bf16),
            pltpu.VMEM((tokens, depth), bf16),
            pltpu.VMEM((nz, local_tokens, depth), bf16),
            pltpu.VMEM((rows, depth), f32),
            pltpu.VMEM((count, PACK, kept), f32),
            pltpu.VMEM((groups, tokens, LANES), f32),
            pltpu.VMEM((tokens, width), bf16),
            pltpu.VMEM((tokens, kept), f32),
            pltpu.VMEM((tokens, LANES), f32),
            pltpu.VMEM((tokens, LANES), f32),
            pltpu.VMEM((tokens, LANES), f32),
            pltpu.VMEM((8, tokens), f32),
            pltpu.VMEM((nv, 8, tokens), f32),
            pltpu.VMEM((nd, 8, tokens), f32),
            pltpu.VMEM((2, half, CHUNK), f32),
            pltpu.VMEM((2, half, CHUNK), bf16),
            pltpu.VMEM((2, half, CHUNK), bf16),
            pltpu.VMEM((2, rows, CHUNK), f32),
            pltpu.VMEM((2, nz, local_tokens, CHUNK), f32),
            pltpu.VMEM((chunks, nz, local_tokens, CHUNK), f32),
            sems(pl.cdiv(width, BLOCK)),
            sems(nz), sems(nz), sems(nz), sems(nz),
            sems(nd), sems(nd), sems(nd), sems(nd),
            sems(nd), sems(nd), sems(nd), sems(nd),
            sems(nv), sems(nv), sems(nd), sems(nd),
            sems(chunks), sems(chunks),
            sems(chunks, nd), sems(chunks, nd),
            sems(chunks, nz), sems(chunks, nz),
        ],
        compiler_params=pltpu.CompilerParams(
            collective_id=0, has_side_effects=True, vmem_limit_bytes=64 * 1024 * 1024),
        cost_estimate=pl.CostEstimate(
            flops=4 * tokens * depth * width, bytes_accessed=2 * depth * width,
            transcendentals=2 * tokens * width),
        name="fused_head",
    )(hidden, teacher_ids, teacher_probs, target_ids, head_weight.T)
    return loss[:, 0], grad


def solution(mesh):
    in_specs = (
        P(AXES, None),
        P(None, AXES),
        P(AXES, None),
        P(AXES, None),
        P(AXES),
    )
    out_specs = (P(AXES), P(AXES, None))
    return jax.shard_map(
        functools.partial(per_device, mesh.shape["dp"], mesh.shape["vocab"]),
        mesh=mesh, in_specs=in_specs, out_specs=out_specs, check_vma=False
    )
```

time: 123 us -> 77.7 us (0.63)
  Pallas kernels: 108 us -> 74.2 us
  local copies, waits for them, and re-layouts: 8.24 us -> 2.65 us
  other arithmetic: 5.27 us -> 0 us
    pallas_call x4 -> x1, Pallas kernels: 108 us -> 74.2 us  [per_device(): pl.pallas_call(functools.partial(fused_kernel, nd, nv), in_specs=[vmem, v...]
    reshape x4 -> x0, local copies, waits for them, and re-layouts: 4.48 us -> none  [the longest x1 1.95 us: per_device(): all_hidden = got[0].reshape(tokens, depth)]
    convert_element_type x1 -> x0, other arithmetic: 2.36 us -> none  [per_device(): (scale[:, None] * acc[:tokens] - LOSS_SCALE * acc[tokens:]).astype(jnp.bf...]
    unnamed x0 -> x1, local copies, waits for them, and re-layouts: none -> 1.37 us
where the time goes in v1:
time: 77.7 us; the launch traced here: 77.5 us
  Pallas kernels  74.2 us (95%)
  local copies, waits for them, and re-layouts  2.65 us (3%)
    pallas_call x1, Pallas kernels, per_device(): pl.pallas_call(functools.partial(fused_kernel, nd, nv), in_specs=[vmem, v...  74.2 us

profile of v1, /device:TPU:0, one launch (start us, length us, event | category | flops | bytes accessed | tf_op | source)
XLA Modules:
  0.0 77.5 jit_solution(13507354895560345169)
XLA Ops:
  0.6 74.2 %fused_head.1 = (f32[4,128]{1,0:T(4,128)}, bf16[4,3584]{1,0:T(4,128)(2,1)}) custom-call(bf16[4,3584]{1,0:T(4,128)(2,1)} %hid_in.1, s32[4,128]{1,0:T(4,128)} %ids_in.1, f32[4,128]{1,0:T(4,128)} %probs_in.1, s32[4]{0:T(128)} %targets_in.1, bf16[8000,3584]{1,0:T(8,128)(2,1)} %bitcast.1), custom_call_target="tpu_custom_call" | custom-call | flops 14680064000 | bytes 57344000 | tf_op jit(solution)/shard_map/fused_head/pallas_call | solution.py:331
  74.8 1.3 %slice_reduce_fusion = f32[4]{0:T(128)} fusion(f32[4,128]{1,0:T(4,128)} %get-tuple-element.4), kind=kLoop, calls=%fused_computation | loop fusion | bytes 32 | tf_op jit(solution)/shard_map/slice | solution.py:375
  76.1 1.4 %copy.8 = bf16[4,3584]{1,0:T(4,128)(2,1)} copy(bf16[4,3584]{1,0:T(4,128)(2,1)} %get-tuple-element.9) | data formatting | bytes 57344

commit v2 on v1

v2 whole, which is shorter than its diff:
```python
import functools
import jax
import jax.numpy as jnp
from jax import lax
from jax.experimental import pallas as pl
from jax.experimental.pallas import tpu as pltpu
from jax.sharding import PartitionSpec as P

SOFT_CAP = 30.0
CE_WEIGHT = 0.5
LOSS_SCALE = 8.0
BLOCK = 640
CHUNK = 768
LANES = 128
PIECES = 2
LAG = 2
AXES = ("dp", "vocab")
MESH = pl.DeviceIdType.MESH
NT = (((1,), (1,)), ((), ()))


def remote(src, dst, send, recv, peer):
    return pltpu.make_async_remote_copy(
        src_ref=src, dst_ref=dst, send_sem=send, recv_sem=recv,
        device_id=peer, device_id_type=MESH)


def fused_kernel(nd, nv, hid_hbm, ids_hbm, probs_hbm, targets_hbm, w_hbm, out_hbm,
                 ids_in, probs_in, targets_in, out_ref, in_sem, out_sem, w_ref, hid, near, small, cells, grads, probs, exp_part, dot_part,
                 column, totals, slots_v, slots_d, recv3,
                 w_sem, zs_send, zs_recv, zh_send, zh_recv, ds_send, ds_recv, dh_send, dh_recv,
                 cs_send, cs_recv, ch_send, ch_recv, tv_send, tv_recv, td_send, td_recv,
                 r1_send, r1_recv, r2_send, r2_recv, r3_send, r3_recv):
    local_tokens, depth = hid_hbm.shape
    tokens = hid.shape[0]
    width = w_ref.shape[0]
    kept = ids_in.shape[1]
    nz = nv // 2
    rows = nz * local_tokens
    half = nd * rows
    starts = range(0, depth, CHUNK)
    chunks = len(starts)
    d, v = lax.axis_index("dp"), lax.axis_index("vocab")
    z, k = v // 2, lax.rem(v, 2)
    mine = d * 2 + k
    zs = [lax.rem(z + o, nz) for o in range(1, nz)]
    dps = [lax.rem(d + o, nd) for o in range(1, nd)]
    sibling = (d, z * 2 + 1 - k)
    z_peer = lambda q: (d, q * 2 + k)
    d_peer = lambda q: (q, v)

    full_blocks, tail = width // BLOCK, width % BLOCK
    pieces = full_blocks + (tail > 0)

    inputs = [
        pltpu.make_async_copy(src, dst, in_sem.at[i])
        for i, (src, dst) in enumerate((
            (ids_hbm, ids_in), (probs_hbm, probs_in), (targets_hbm, targets_in),
            (hid_hbm, near.at[z])))
    ]
    for copy in inputs:
        copy.start()

    barrier = pltpu.get_barrier_semaphore()
    peers_v = [(d, lax.rem(v + o, nv)) for o in range(1, nv)]
    peers_d = [d_peer(q) for q in dps]
    for peer in peers_v + peers_d:
        pl.semaphore_signal(barrier, inc=1, device_id=peer, device_id_type=MESH)

    def w_copy(j, size):
        at = pl.ds(pl.multiple_of(j * BLOCK, BLOCK), size)
        return pltpu.make_async_copy(w_hbm.at[at], w_ref.at[at], w_sem.at[j])

    def start_w(j, carry):
        w_copy(j, BLOCK).start()
        return carry

    lax.fori_loop(0, full_blocks, start_w, 0)
    if tail:
        w_copy(full_blocks, tail).start()

    for copy in inputs:
        copy.wait()
    own_block = mine * nz + z
    lane = lax.broadcasted_iota(jnp.int32, (1, kept), 1)
    target_row = jnp.zeros((1, kept), jnp.int32)
    for i in range(local_tokens):
        target_row = jnp.where(lane == i, targets_in[i], target_row)
    small[own_block, 0:local_tokens, :] = ids_in[...].astype(jnp.float32)
    small[own_block, local_tokens:2 * local_tokens, :] = probs_in[...]
    small[own_block, 2 * local_tokens:, :] = target_row.astype(jnp.float32)

    pl.semaphore_wait(barrier, nv + nd - 2)

    sent = []
    part = depth // PIECES

    def go(copy):
        copy.start()
        sent.append(copy)

    def small_at(group):
        return small.at[pl.ds(group * nz, nz)]

    def hid_at(group, p):
        return hid.at[pl.ds(pl.multiple_of(group * rows, rows), rows), pl.ds(p * part, part)]

    def near_copy(o, q, source, p):
        at = pl.ds(p * part, part)
        return remote(near.at[source, :, at], near.at[source, :, at],
                      zh_send.at[p, o], zh_recv.at[p, source], z_peer(q))

    def to_sibling(source, p):
        at = hid_at(source * 2 + k, p)
        go(remote(at, at, ch_send.at[p, source], ch_recv.at[p, source], sibling))

    def to_dp(o, q, p):
        at = hid_at(mine, p)
        go(remote(at, at, dh_send.at[p, o], dh_recv.at[p, d], d_peer(q)))

    def from_dp(source, p):
        at = hid_at(source * 2 + k, p)
        remote(at, at, dh_send.at[p, 0], dh_recv.at[p, source], d_peer(source)).wait_recv()

    for o, q in enumerate(zs):
        go(remote(small.at[own_block], small.at[own_block], zs_send.at[o], zs_recv.at[z],
                  z_peer(q)))
    for p in range(PIECES):
        for o, q in enumerate(zs):
            go(near_copy(o, q, z, p))
    for o, q in enumerate(zs):
        at = small.at[mine * nz + q]
        remote(at, at, zs_send.at[o], zs_recv.at[q], z_peer(q)).wait_recv()
    at = small_at(mine)
    for o, q in enumerate(dps):
        go(remote(at, at, ds_send.at[o], ds_recv.at[d], d_peer(q)))
    go(remote(at, at, cs_send.at[d], cs_recv.at[d], sibling))

    for p in range(PIECES):
        at = pl.ds(p * part, part)
        for o, q in enumerate(zs):
            near_copy(o, q, q, p).wait_recv()

        def lay_out(near32):
            for q in range(nz):
                near32[q * local_tokens:(q + 1) * local_tokens, :] = near[q, :, at].astype(
                    jnp.float32)
            hid[pl.ds(pl.multiple_of(mine * rows, rows), rows), at] = near32[...].astype(
                jnp.bfloat16)

        pl.run_scoped(lay_out, pltpu.VMEM((rows, part), jnp.float32))
        for o, q in enumerate(dps):
            to_dp(o, q, p)
        to_sibling(d, p)

    for o, q in enumerate(dps):
        at = small_at(q * 2 + k)
        remote(at, at, ds_send.at[o], ds_recv.at[q], d_peer(q)).wait_recv()
        go(remote(at, at, cs_send.at[q], cs_recv.at[q], sibling))

    groups = pl.cdiv(width, LANES)
    group_rows = 16 * pl.cdiv(groups, 16)
    offset = (d * nv + v) * width
    group_row = lax.broadcasted_iota(jnp.int32, (group_rows, kept), 0)
    lane_row = lax.broadcasted_iota(jnp.int32, (LANES, kept), 0)
    flat = group_row * LANES + lax.broadcasted_iota(jnp.int32, (group_rows, LANES), 1)
    per_step = 8 // local_tokens

    def scatter(step, carry):
        first = pl.multiple_of(step * 8, 8)
        found = []
        for i in range(8):
            block = step * per_step + i // local_tokens
            r = i % local_tokens
            ids = small[block, r:r + 1, :].astype(jnp.int32) - offset
            p = small[block, local_tokens + r:local_tokens + r + 1, :]
            target = small[block, 2 * local_tokens:, r:r + 1].astype(jnp.int32) - offset
            probs[pl.ds(first + i, 1), :] = p
            high = p.astype(jnp.bfloat16).astype(jnp.float32)
            inside = group_row == (ids >> 7)
            left = jnp.concatenate(
                [jnp.where(inside, high, 0.0), jnp.where(inside, p - high, 0.0)],
                axis=0).astype(jnp.bfloat16)
            right = jnp.where(lane_row == (ids & 127), 1.0, 0.0).astype(jnp.bfloat16)
            both = lax.dot_general(left, right, NT, preferred_element_type=jnp.float32)
            found.append(both[:group_rows] + both[group_rows:]
                         + jnp.where(flat == target, CE_WEIGHT, 0.0))
        cells[:, pl.ds(first, 8), :] = jnp.swapaxes(jnp.stack(found, axis=0), 0, 1)[:groups]
        return carry

    steps = tokens // 8 // PIECES
    for p in range(PIECES):
        for o, q in enumerate(dps):
            from_dp(q, p)
            to_sibling(q, p)
        if p == 0:
            for q in range(nd):
                at = small_at(q * 2 + 1 - k)
                remote(at, at, cs_send.at[q], cs_recv.at[q], sibling).wait_recv()
        lax.fori_loop(p * steps, (p + 1) * steps, scatter, 0)
    for p in range(PIECES):
        for q in range(nd):
            at = hid_at(q * 2 + 1 - k, p)
            remote(at, at, ch_send.at[p, q], ch_recv.at[p, q], sibling).wait_recv()
    for copy in sent:
        copy.wait_send()
    sent.clear()

    exp_part[...] = jnp.zeros_like(exp_part)
    dot_part[...] = jnp.zeros_like(dot_part)

    def finish_block(j, size, logits):
        for i in range(pl.cdiv(size, LANES)):
            n = min(LANES, size - i * LANES)
            group = j * (BLOCK // LANES) + i
            ratio = jnp.tanh(logits[:, i * LANES:i * LANES + n] * (1.0 / SOFT_CAP))
            capped = SOFT_CAP * ratio
            slope = 1.0 - ratio * ratio
            exps = jnp.exp(capped)
            sparse = cells[group, :, 0:n]
            cells[group, :, 0:n] = exps * slope
            grads[:, pl.ds(pl.multiple_of(group * LANES, LANES), n)] = (
                sparse * slope).astype(jnp.bfloat16)
            exp_part[:, 0:n] += exps
            dot_part[:, 0:n] += capped * sparse

    def raw_block(j, size):
        w = w_ref[pl.ds(pl.multiple_of(j * BLOCK, BLOCK), size), :]
        return lax.dot_general(w, hid[...], NT, preferred_element_type=jnp.float32)

    def all_blocks(raw):
        w_copy(0, BLOCK).wait()
        raw[0] = raw_block(0, BLOCK)

        def full_block(j, carry):
            w_copy(j, BLOCK).wait()
            finish_block(j - 1, BLOCK, raw[lax.rem(j + 1, 2)].T)
            raw[lax.rem(j, 2)] = raw_block(j, BLOCK)
            return carry

        lax.fori_loop(1, full_blocks, full_block, 0)
        previous = raw[(full_blocks - 1) % 2].T
        if tail:
            w_copy(full_blocks, tail).wait()
            logits = raw_block(full_blocks, tail).T
            finish_block(full_blocks - 1, BLOCK, previous)
            finish_block(full_blocks, tail, logits)
        else:
            finish_block(full_blocks - 1, BLOCK, previous)

    pl.run_scoped(all_blocks, pltpu.VMEM((2, BLOCK, tokens), jnp.float32))

    def cols(i):
        return pl.ds(starts[i], min(CHUNK, depth - starts[i]))

    def copy1(i, send):
        return remote(send.at[:, cols(i)], hid.at[pl.ds(0, half), cols(i)],
                      r1_send.at[i], r1_recv.at[i], sibling)

    def copy2(i, send, o, q, source):
        return remote(send.at[pl.ds(pl.multiple_of(q * rows, rows), rows), cols(i)],
                      hid.at[pl.ds(pl.multiple_of(half + source * rows, rows), rows), cols(i)],
                      r2_send.at[i, o], r2_recv.at[i, source], d_peer(q))

    def copy3(i, send3, o, q, source):
        return remote(send3.at[q, :, cols(i)], recv3.at[source, :, cols(i)],
                      r3_send.at[i, o], r3_recv.at[i, source], z_peer(q))

    def out_copy(start, size, sem):
        at = pl.ds(start, size)
        return pltpu.make_async_copy(out_ref.at[:, at], out_hbm.at[:, at], sem)

    def exp_product(i):
        total = None
        for first in range(0, groups, 8):
            last = min(groups, first + 8)
            rows_w = slice(first * LANES, min(width, last * LANES))
            left = jnp.concatenate([cells[g] for g in range(first, last)], axis=1)
            left = left[:, :rows_w.stop - rows_w.start].astype(jnp.bfloat16)
            term = jnp.dot(left, w_ref[rows_w, cols(i)], preferred_element_type=jnp.float32)
            total = term if total is None else total + term
        return total

    def grad_product(i):
        return jnp.dot(grads[...], w_ref[:, cols(i)], preferred_element_type=jnp.float32)

    def exchange_start(peers, me, slots, send, recv):
        slots[me] = totals[...]
        for o, peer in enumerate(peers):
            go(remote(slots.at[me], slots.at[me], send.at[o], recv.at[me], peer))

    def exchange_end(peers, slots, send, recv, axis):
        for o, peer in enumerate(peers):
            at = slots.at[peer[axis]]
            remote(at, at, send.at[o], recv.at[peer[axis]], peer).wait_recv()
        totals[...] = jnp.sum(slots[...], axis=0)

    def scale_group(group, n):
        at = pl.ds(pl.multiple_of(group * LANES, LANES), n)
        grads[:, at] = (column[:, 0:n] * cells[group, :, 0:n]
                        - LOSS_SCALE * grads[:, at].astype(jnp.float32)).astype(jnp.bfloat16)

    def scale_full(group, carry):
        scale_group(group, LANES)
        return carry

    def sum_chunks(own1, own2, send, send3):
        totals[...] = jnp.zeros_like(totals)
        totals[0:1, :] = jnp.sum(exp_part[...].T, axis=0, keepdims=True)
        totals[1:2, :] = jnp.sum(dot_part[...].T, axis=0, keepdims=True)
        exchange_start(peers_v, v, slots_v, tv_send, tv_recv)
        term = exp_product(0)
        own1[0] = term[:half]
        own1[1] = term[half:]
        exchange_end(peers_v, slots_v, tv_send, tv_recv, 1)
        exchange_start(peers_d, d, slots_d, td_send, td_recv)
        term = grad_product(0)
        exchange_end(peers_d, slots_d, td_send, td_recv, 0)

        spread = lambda row: jnp.broadcast_to(row, (LANES, tokens)).T
        exp_sum = spread(totals[0:1, :])
        exp_part[...] = exp_sum
        dot_part[...] = spread(totals[1:2, :])
        teacher_sum = jnp.sum(probs[...], axis=1, keepdims=True)
        scale = LOSS_SCALE * (teacher_sum + CE_WEIGHT) / exp_sum
        column[...] = scale

        def sum_cores(i, acc):
            size = acc.shape[1]
            acc = acc.reshape(nd, 2, rows, size)
            own1[i % 2, :, 0:size] = jnp.where(k == 0, acc[:, 0], acc[:, 1]).reshape(half, size)
            send[:, cols(i)] = jnp.where(k == 0, acc[:, 1], acc[:, 0]).reshape(half, size).astype(
                jnp.bfloat16)
            copy1(i, send).start()

        def sum_dp(i):
            size = cols(i).size
            copy1(i, send).wait()
            total = own1[i % 2, :, 0:size] + hid[0:half, cols(i)].astype(jnp.float32)
            send[:, cols(i)] = total.astype(jnp.bfloat16)
            for o, q in enumerate(dps):
                copy2(i, send, o, q, d).start()
            own1[i % 2, :, 0:size] = total
            own2[:, cols(i)] = own1[i % 2, pl.ds(pl.multiple_of(d * rows, rows), rows), 0:size]

        def sum_z(i):
            total = own2[:, cols(i)]
            for o, q in enumerate(dps):
                copy2(i, send, o, q, q).wait_recv()
                at = pl.ds(pl.multiple_of(half + q * rows, rows), rows)
                total = total + hid[at, cols(i)].astype(jnp.float32)
            for q in range(nz):
                send3[q, :, cols(i)] = total[q * local_tokens:(q + 1) * local_tokens]
            for o, q in enumerate(zs):
                copy3(i, send3, o, q, z).start()
            recv3[z, :, cols(i)] = send3[z, :, cols(i)]

        def put_out(i):
            for o, q in enumerate(zs):
                copy3(i, send3, o, q, q).wait_recv()
            total = recv3[0, :, cols(i)]
            for q in range(1, nz):
                total = total + recv3[q, :, cols(i)]
            out_ref[:, cols(i)] = total
            out_copy(starts[i], cols(i).size, out_sem.at[i]).start()

        size = cols(0).size
        first = jnp.concatenate([own1[0, :, 0:size], own1[1, :, 0:size]], axis=0)
        sum_cores(0, jnp.concatenate(
            [scale * first[:, at:at + LANES] - LOSS_SCALE * term[:, at:at + LANES]
             for at in range(0, size, LANES)], axis=1))
        lax.fori_loop(0, width // LANES, scale_full, 0)
        if width % LANES:
            scale_group(width // LANES, width % LANES)

        for i in range(chunks + 1 + 2 * LAG):
            if 0 < i < chunks:
                sum_cores(i, grad_product(i))
            if i == 1:
                own_row = mine * rows + z * local_tokens
                for r in range(local_tokens):
                    p = probs_in[r:r + 1, :]
                    out_ref[r:r + 1, depth:] = (
                        jnp.sum(p * jnp.log(p), axis=1, keepdims=True)
                        - dot_part[pl.ds(own_row + r, 1), :]
                        + (jnp.sum(p, axis=1, keepdims=True) + CE_WEIGHT)
                        * jnp.log(exp_part[pl.ds(own_row + r, 1), :]))
                out_copy(depth, LANES, out_sem.at[chunks]).start()
            if 0 <= i - 1 < chunks:
                sum_dp(i - 1)
            if 0 <= i - 1 - LAG < chunks:
                sum_z(i - 1 - LAG)
            if 0 <= i - 1 - 2 * LAG < chunks:
                put_out(i - 1 - 2 * LAG)

        for copy in sent:
            copy.wait_send()
        for i in range(chunks):
            for o, q in enumerate(dps):
                copy2(i, send, o, q, d).wait_send()
            for o, q in enumerate(zs):
                copy3(i, send3, o, q, z).wait_send()
            out_copy(starts[i], cols(i).size, out_sem.at[i]).wait()
        out_copy(depth, LANES, out_sem.at[chunks]).wait()

    pl.run_scoped(
        sum_chunks,
        pltpu.VMEM((2, half, CHUNK), jnp.float32),
        pltpu.VMEM((rows, depth), jnp.float32),
        pltpu.VMEM((half, depth), jnp.bfloat16),
        pltpu.VMEM((nz, local_tokens, depth), jnp.float32))


def per_device(nd, nv, hidden, head_weight, teacher_ids, teacher_probs, target_ids):
    local_tokens, depth = hidden.shape
    width = head_weight.shape[1]
    kept = teacher_ids.shape[1]
    count = nd * nv
    tokens = count * local_tokens
    nz = nv // 2
    rows = nz * local_tokens
    half = nd * rows
    chunks = pl.cdiv(depth, CHUNK)
    groups = pl.cdiv(width, LANES)
    f32, bf16 = jnp.float32, jnp.bfloat16
    sems = lambda *shape: pltpu.SemaphoreType.DMA(shape)
    hbm = pl.BlockSpec(memory_space=pl.ANY)
    out = pl.pallas_call(
        functools.partial(fused_kernel, nd, nv),
        in_specs=[hbm] * 5,
        out_specs=hbm,
        out_shape=jax.ShapeDtypeStruct((local_tokens, depth + LANES), f32),
        scratch_shapes=[
            pltpu.VMEM((local_tokens, kept), jnp.int32),
            pltpu.VMEM((local_tokens, kept), f32),
            pltpu.SMEM((local_tokens,), jnp.int32),
            pltpu.VMEM((local_tokens, depth + LANES), f32),
            sems(4),
            sems(chunks + 1),
            pltpu.VMEM((width, depth), bf16),
            pltpu.VMEM((tokens, depth), bf16),
            pltpu.VMEM((nz, local_tokens, depth), bf16),
            pltpu.VMEM((count, 2 * local_tokens + 1, kept), f32),
            pltpu.VMEM((groups, tokens, LANES), f32),
            pltpu.VMEM((tokens, width), bf16),
            pltpu.VMEM((tokens, kept), f32),
            pltpu.VMEM((tokens, LANES), f32),
            pltpu.VMEM((tokens, LANES), f32),
            pltpu.VMEM((tokens, LANES), f32),
            pltpu.VMEM((8, tokens), f32),
            pltpu.VMEM((nv, 8, tokens), f32),
            pltpu.VMEM((nd, 8, tokens), f32),
            pltpu.VMEM((nz, local_tokens, depth), f32),
            sems(pl.cdiv(width, BLOCK)),
            sems(nz), sems(nz), sems(PIECES, nz), sems(PIECES, nz),
            sems(nd), sems(nd), sems(PIECES, nd), sems(PIECES, nd),
            sems(nd), sems(nd), sems(PIECES, nd), sems(PIECES, nd),
            sems(nv), sems(nv), sems(nd), sems(nd),
            sems(chunks), sems(chunks),
            sems(chunks, nd), sems(chunks, nd),
            sems(chunks, nz), sems(chunks, nz),
        ],
        compiler_params=pltpu.CompilerParams(
            collective_id=0, has_side_effects=True, vmem_limit_bytes=64 * 1024 * 1024),
        cost_estimate=pl.CostEstimate(
            flops=4 * tokens * depth * width, bytes_accessed=2 * depth * width,
            transcendentals=2 * tokens * width),
        name="fused_head",
    )(hidden, teacher_ids, teacher_probs, target_ids, head_weight.T)
    return out[:, depth], out[:, :depth].astype(bf16)


def solution(mesh):
    in_specs = (
        P(AXES, None),
        P(None, AXES),
        P(AXES, None),
        P(AXES, None),
        P(AXES),
    )
    out_specs = (P(AXES), P(AXES, None))
    return jax.shard_map(
        functools.partial(per_device, mesh.shape["dp"], mesh.shape["vocab"]),
        mesh=mesh, in_specs=in_specs, out_specs=out_specs, check_vma=False
    )
```

time: 77.7 us -> 69.5 us (0.89)
  Pallas kernels: 74.2 us -> 66 us
    pallas_call x1, Pallas kernels: 74.2 us -> 66 us  [per_device(): pl.pallas_call(functools.partial(fused_kernel, nd, nv), in_specs=[hbm] *...]
    slice x1 -> x2, local copies, waits for them, and re-layouts: 1.28 us -> 2.74 us  [per_device(): return (out[:, depth], out[:, :depth].astype(bf16))]
    unnamed x1 -> x0, local copies, waits for them, and re-layouts: 1.37 us -> none
where the time goes in v2:
time: 69.5 us; the launch traced here: 69.3 us
  Pallas kernels  66 us (95%)
  local copies, waits for them, and re-layouts  2.74 us (4%)
    pallas_call x1, Pallas kernels, per_device(): pl.pallas_call(functools.partial(fused_kernel, nd, nv), in_specs=[hbm] *...  66 us
    slice x2, local copies, waits for them, and re-layouts, per_device(): return (out[:, depth], out[:, :depth].astype(bf16))  2.74 us

profile of v2, /device:TPU:0, one launch (start us, length us, event | category | flops | bytes accessed | tf_op | source)
XLA Modules:
  0.0 69.3 jit_solution(16909613984492478856)
XLA Ops:
  0.6 66.0 %fused_head.1 = f32[4,3712]{1,0:T(4,128)} custom-call(bf16[4,3584]{1,0:T(4,128)(2,1)} %hid_hbm.1, s32[4,128]{1,0:T(4,128)} %ids_hbm.1, f32[4,128]{1,0:T(4,128)} %probs_hbm.1, s32[4]{0:T(128)} %targets_hbm.1, bf16[8000,3584]{1,0:T(8,128)(2,1)} %bitcast.1), custom_call_target="tpu_custom_call" | custom-call | flops 14680064000 | bytes 57344000 | tf_op jit(solution)/shard_map/fused_head/pallas_call | solution.py:428
  66.6 1.3 %slice_reduce_fusion = f32[4]{0:T(128)} fusion(f32[4,3712]{1,0:T(4,128)} %fused_head.1), kind=kLoop, calls=%fused_computation.1 | loop fusion | bytes 32 | tf_op jit(solution)/shard_map/slice | solution.py:470
  67.9 1.4 %slice.12 = bf16[4,3584]{1,0:T(4,128)(2,1)} slice(f32[4,3712]{1,0:T(4,128)} %fused_head.1), slice={[0:4], [0:3584]} | slice | bytes 57344 | tf_op jit(solution)/shard_map/slice | solution.py:470

commit v3 on v2

--- a/solution.py
+++ b/solution.py
@@ -26,10 +26,11 @@
 
 
 def fused_kernel(nd, nv, hid_hbm, ids_hbm, probs_hbm, targets_hbm, w_hbm, out_hbm,
-                 ids_in, probs_in, targets_in, out_ref, in_sem, out_sem, w_ref, hid, near, small, cells, grads, probs, exp_part, dot_part,
-                 column, totals, slots_v, slots_d, recv3,
+                 ids_in, probs_in, targets_in, out_ref, in_sem, out_sem, w_ref, hid, small, cells, grads, probs, exp_part, dot_part,
+                 slots, near,
+                 direct_send, direct_recv, direct_sems,
                  w_sem, zs_send, zs_recv, zh_send, zh_recv, ds_send, ds_recv, dh_send, dh_recv,
-                 cs_send, cs_recv, ch_send, ch_recv, tv_send, tv_recv, td_send, td_recv,
+                 cs_send, cs_recv, ch_send, ch_recv, t_send, t_recv,
                  r1_send, r1_recv, r2_send, r2_recv, r3_send, r3_recv):
     local_tokens, depth = hid_hbm.shape
     tokens = hid.shape[0]
@@ -62,9 +63,8 @@
         copy.start()
 
     barrier = pltpu.get_barrier_semaphore()
-    peers_v = [(d, lax.rem(v + o, nv)) for o in range(1, nv)]
-    peers_d = [d_peer(q) for q in dps]
-    for peer in peers_v + peers_d:
+    peers = [(lax.rem(d + o // nv, nd), lax.rem(v + o % nv, nv)) for o in range(1, nd * nv)]
+    for peer in peers:
         pl.semaphore_signal(barrier, inc=1, device_id=peer, device_id_type=MESH)
 
     def w_copy(j, size):
@@ -90,7 +90,7 @@
     small[own_block, local_tokens:2 * local_tokens, :] = probs_in[...]
     small[own_block, 2 * local_tokens:, :] = target_row.astype(jnp.float32)
 
-    pl.semaphore_wait(barrier, nv + nd - 2)
+    pl.semaphore_wait(barrier, nd * nv - 1)
 
     sent = []
     part = depth // PIECES
@@ -188,23 +188,23 @@
         cells[:, pl.ds(first, 8), :] = jnp.swapaxes(jnp.stack(found, axis=0), 0, 1)[:groups]
         return carry
 
-    steps = tokens // 8 // PIECES
+    for q in range(nd):
+        at = small_at(q * 2 + 1 - k)
+        remote(at, at, cs_send.at[q], cs_recv.at[q], sibling).wait_recv()
+    steps = tokens // 8
+    marks = [0, steps * 3 // 8, steps * 7 // 8, steps]
+    lax.fori_loop(marks[0], marks[1], scatter, 0, unroll=2)
     for p in range(PIECES):
         for o, q in enumerate(dps):
             from_dp(q, p)
             to_sibling(q, p)
-        if p == 0:
-            for q in range(nd):
-                at = small_at(q * 2 + 1 - k)
-                remote(at, at, cs_send.at[q], cs_recv.at[q], sibling).wait_recv()
-        lax.fori_loop(p * steps, (p + 1) * steps, scatter, 0)
-    for p in range(PIECES):
+        lax.fori_loop(marks[p + 1], marks[p + 2], scatter, 0, unroll=2)
+    def from_sibling(p):
         for q in range(nd):
             at = hid_at(q * 2 + 1 - k, p)
             remote(at, at, ch_send.at[p, q], ch_recv.at[p, q], sibling).wait_recv()
-    for copy in sent:
-        copy.wait_send()
-    sent.clear()
+
+    from_sibling(0)
 
     exp_part[...] = jnp.zeros_like(exp_part)
     dot_part[...] = jnp.zeros_like(dot_part)
@@ -228,9 +228,20 @@
         w = w_ref[pl.ds(pl.multiple_of(j * BLOCK, BLOCK), size), :]
         return lax.dot_general(w, hid[...], NT, preferred_element_type=jnp.float32)
 
+    def piece_product(j, p):
+        at = slice(p * part, (p + 1) * part)
+        return lax.dot_general(w_ref[j * BLOCK:(j + 1) * BLOCK, at], hid[:, at], NT,
+                               preferred_element_type=jnp.float32)
+
     def all_blocks(raw):
-        w_copy(0, BLOCK).wait()
-        raw[0] = raw_block(0, BLOCK)
+        for j in range(2):
+            w_copy(j, BLOCK).wait()
+            raw[j] = piece_product(j, 0)
+        for p in range(1, PIECES):
+            from_sibling(p)
+        raw[0] += sum(piece_product(0, p) for p in range(1, PIECES))
+        finish_block(0, BLOCK, raw[0].T)
+        raw[1] += sum(piece_product(1, p) for p in range(1, PIECES))
 
         def full_block(j, carry):
             w_copy(j, BLOCK).wait()
@@ -238,7 +249,7 @@
             raw[lax.rem(j, 2)] = raw_block(j, BLOCK)
             return carry
 
-        lax.fori_loop(1, full_blocks, full_block, 0)
+        lax.fori_loop(2, full_blocks, full_block, 0)
         previous = raw[(full_blocks - 1) % 2].T
         if tail:
             w_copy(full_blocks, tail).wait()
@@ -249,6 +260,8 @@
             finish_block(full_blocks - 1, BLOCK, previous)
 
     pl.run_scoped(all_blocks, pltpu.VMEM((2, BLOCK, tokens), jnp.float32))
+    for copy in sent:
+        copy.wait_send()
 
     def cols(i):
         return pl.ds(starts[i], min(CHUNK, depth - starts[i]))
@@ -263,7 +276,7 @@
                       r2_send.at[i, o], r2_recv.at[i, source], d_peer(q))
 
     def copy3(i, send3, o, q, source):
-        return remote(send3.at[q, :, cols(i)], recv3.at[source, :, cols(i)],
+        return remote(send3.at[q, :, cols(i)], near.at[source, :, cols(i)],
                       r3_send.at[i, o], r3_recv.at[i, source], z_peer(q))
 
     def out_copy(start, size, sem):
@@ -284,20 +297,19 @@
     def grad_product(i):
         return jnp.dot(grads[...], w_ref[:, cols(i)], preferred_element_type=jnp.float32)
 
-    def exchange_start(peers, me, slots, send, recv):
-        slots[me] = totals[...]
-        for o, peer in enumerate(peers):
-            go(remote(slots.at[me], slots.at[me], send.at[o], recv.at[me], peer))
-
-    def exchange_end(peers, slots, send, recv, axis):
-        for o, peer in enumerate(peers):
-            at = slots.at[peer[axis]]
-            remote(at, at, send.at[o], recv.at[peer[axis]], peer).wait_recv()
-        totals[...] = jnp.sum(slots[...], axis=0)
+    twins = [(lax.rem(d + o // nz, nd), lax.rem(z + o % nz, nz)) for o in range(1, nd * nz)]
+
+    def direct_copy(o, peer_d, peer_z, source):
+        return remote(direct_send.at[peer_d * nz + peer_z], direct_recv.at[source],
+                      direct_sems.at[0, o], direct_sems.at[1, source], (peer_d, peer_z * 2 + k))
+
+    def total_copy(o, peer, source):
+        at = slots.at[source]
+        return remote(at, at, t_send.at[o], t_recv.at[source], peer)
 
     def scale_group(group, n):
         at = pl.ds(pl.multiple_of(group * LANES, LANES), n)
-        grads[:, at] = (column[:, 0:n] * cells[group, :, 0:n]
+        grads[:, at] = (probs[:, 0:n] * cells[group, :, 0:n]
                         - LOSS_SCALE * grads[:, at].astype(jnp.float32)).astype(jnp.bfloat16)
 
     def scale_full(group, carry):
@@ -305,17 +317,19 @@
         return carry
 
     def sum_chunks(own1, own2, send, send3):
-        totals[...] = jnp.zeros_like(totals)
-        totals[0:1, :] = jnp.sum(exp_part[...].T, axis=0, keepdims=True)
-        totals[1:2, :] = jnp.sum(dot_part[...].T, axis=0, keepdims=True)
-        exchange_start(peers_v, v, slots_v, tv_send, tv_recv)
+        here = d * nv + v
+        slots[here] = jnp.concatenate(
+            [jnp.sum(exp_part[...].T, axis=0, keepdims=True),
+             jnp.sum(dot_part[...].T, axis=0, keepdims=True)], axis=0)
+        for o, peer in enumerate(peers):
+            total_copy(o, peer, here).start()
         term = exp_product(0)
         own1[0] = term[:half]
         own1[1] = term[half:]
-        exchange_end(peers_v, slots_v, tv_send, tv_recv, 1)
-        exchange_start(peers_d, d, slots_d, td_send, td_recv)
         term = grad_product(0)
-        exchange_end(peers_d, slots_d, td_send, td_recv, 0)
+        for o, (peer_d, peer_v) in enumerate(peers):
+            total_copy(o, (peer_d, peer_v), peer_d * nv + peer_v).wait_recv()
+        totals = jnp.sum(slots[...], axis=0)
 
         spread = lambda row: jnp.broadcast_to(row, (LANES, tokens)).T
         exp_sum = spread(totals[0:1, :])
@@ -323,7 +337,7 @@
         dot_part[...] = spread(totals[1:2, :])
         teacher_sum = jnp.sum(probs[...], axis=1, keepdims=True)
         scale = LOSS_SCALE * (teacher_sum + CE_WEIGHT) / exp_sum
-        column[...] = scale
+        probs[...] = scale
 
         def sum_cores(i, acc):
             size = acc.shape[1]
@@ -350,19 +364,35 @@
                 at = pl.ds(pl.multiple_of(half + q * rows, rows), rows)
                 total = total + hid[at, cols(i)].astype(jnp.float32)
             for q in range(nz):
-                send3[q, :, cols(i)] = total[q * local_tokens:(q + 1) * local_tokens]
+                send3[q, :, cols(i)] = total[q * local_tokens:(q + 1) * local_tokens].astype(
+                    jnp.bfloat16)
             for o, q in enumerate(zs):
                 copy3(i, send3, o, q, z).start()
-            recv3[z, :, cols(i)] = send3[z, :, cols(i)]
+            near[z, :, cols(i)] = send3[z, :, cols(i)]
 
         def put_out(i):
             for o, q in enumerate(zs):
                 copy3(i, send3, o, q, q).wait_recv()
-            total = recv3[0, :, cols(i)]
-            for q in range(1, nz):
-                total = total + recv3[q, :, cols(i)]
-            out_ref[:, cols(i)] = total
+            out_ref[:, cols(i)] = jnp.sum(near[:, :, cols(i)].astype(jnp.float32), axis=0)
             out_copy(starts[i], cols(i).size, out_sem.at[i]).start()
+
+        def send_last(i):
+            size = cols(i).size
+            copy1(i, send).wait()
+            total = own1[i % 2, :, 0:size] + hid[0:half, cols(i)].astype(jnp.float32)
+            for q in range(nd * nz):
+                direct_send[q, :, 0:size] = total[q * local_tokens:(q + 1) * local_tokens].astype(
+                    jnp.bfloat16)
+            for o, (peer_d, peer_z) in enumerate(twins):
+                direct_copy(o, peer_d, peer_z, d * nz + z).start()
+            direct_recv[d * nz + z] = direct_send[d * nz + z]
+
+        def put_last(i):
+            size = cols(i).size
+            for o, (peer_d, peer_z) in enumerate(twins):
+                direct_copy(o, peer_d, peer_z, peer_d * nz + peer_z).wait_recv()
+            out_ref[:, cols(i)] = jnp.sum(direct_recv[:, :, 0:size].astype(jnp.float32), axis=0)
+            out_copy(starts[i], size, out_sem.at[i]).start()
 
         size = cols(0).size
         first = jnp.concatenate([own1[0, :, 0:size], own1[1, :, 0:size]], axis=0)
@@ -373,7 +403,7 @@
         if width % LANES:
             scale_group(width // LANES, width % LANES)
 
-        for i in range(chunks + 1 + 2 * LAG):
+        for i in range(chunks + 2 * LAG):
             if 0 < i < chunks:
                 sum_cores(i, grad_product(i))
             if i == 1:
@@ -386,20 +416,26 @@
                         + (jnp.sum(p, axis=1, keepdims=True) + CE_WEIGHT)
                         * jnp.log(exp_part[pl.ds(own_row + r, 1), :]))
                 out_copy(depth, LANES, out_sem.at[chunks]).start()
-            if 0 <= i - 1 < chunks:
+            if i == chunks:
+                send_last(i - 1)
+            elif 0 < i < chunks:
                 sum_dp(i - 1)
-            if 0 <= i - 1 - LAG < chunks:
+            if 0 <= i - 1 - LAG < chunks - 1:
                 sum_z(i - 1 - LAG)
-            if 0 <= i - 1 - 2 * LAG < chunks:
+            if 0 <= i - 1 - 2 * LAG < chunks - 1:
                 put_out(i - 1 - 2 * LAG)
-
-        for copy in sent:
-            copy.wait_send()
-        for i in range(chunks):
+        put_last(chunks - 1)
+
+        for o, peer in enumerate(peers):
+            total_copy(o, peer, here).wait_send()
+        for i in range(chunks - 1):
             for o, q in enumerate(dps):
                 copy2(i, send, o, q, d).wait_send()
             for o, q in enumerate(zs):
                 copy3(i, send3, o, q, z).wait_send()
+        for o, (peer_d, peer_z) in enumerate(twins):
+            direct_copy(o, peer_d, peer_z, d * nz + z).wait_send()
+        for i in range(chunks):
             out_copy(starts[i], cols(i).size, out_sem.at[i]).wait()
         out_copy(depth, LANES, out_sem.at[chunks]).wait()
 
@@ -408,7 +444,7 @@
         pltpu.VMEM((2, half, CHUNK), jnp.float32),
         pltpu.VMEM((rows, depth), jnp.float32),
         pltpu.VMEM((half, depth), jnp.bfloat16),
-        pltpu.VMEM((nz, local_tokens, depth), jnp.float32))
+        pltpu.VMEM((nz, local_tokens, depth), jnp.bfloat16))
 
 
 def per_device(nd, nv, hidden, head_weight, teacher_ids, teacher_probs, target_ids):
@@ -439,23 +475,22 @@
             sems(chunks + 1),
             pltpu.VMEM((width, depth), bf16),
             pltpu.VMEM((tokens, depth), bf16),
-            pltpu.VMEM((nz, local_tokens, depth), bf16),
             pltpu.VMEM((count, 2 * local_tokens + 1, kept), f32),
             pltpu.VMEM((groups, tokens, LANES), f32),
             pltpu.VMEM((tokens, width), bf16),
-            pltpu.VMEM((tokens, kept), f32),
             pltpu.VMEM((tokens, LANES), f32),
             pltpu.VMEM((tokens, LANES), f32),
             pltpu.VMEM((tokens, LANES), f32),
-            pltpu.VMEM((8, tokens), f32),
-            pltpu.VMEM((nv, 8, tokens), f32),
-            pltpu.VMEM((nd, 8, tokens), f32),
-            pltpu.VMEM((nz, local_tokens, depth), f32),
+            pltpu.VMEM((count, 2, tokens), f32),
+            pltpu.VMEM((nz, local_tokens, depth), bf16),
+            pltpu.VMEM((nd * nz, local_tokens, (depth - 1) % CHUNK + 1), bf16),
+            pltpu.VMEM((nd * nz, local_tokens, (depth - 1) % CHUNK + 1), bf16),
+            sems(2, nd * nz),
             sems(pl.cdiv(width, BLOCK)),
             sems(nz), sems(nz), sems(PIECES, nz), sems(PIECES, nz),
             sems(nd), sems(nd), sems(PIECES, nd), sems(PIECES, nd),
             sems(nd), sems(nd), sems(PIECES, nd), sems(PIECES, nd),
-            sems(nv), sems(nv), sems(nd), sems(nd),
+            sems(count), sems(count),
             sems(chunks), sems(chunks),
             sems(chunks, nd), sems(chunks, nd),
             sems(chunks, nz), sems(chunks, nz),

time: 69.5 us -> 67.8 us (0.976)
  Pallas kernels: 66 us -> 64.2 us
    pallas_call x1, Pallas kernels: 66 us -> 64.2 us  [per_device(): pl.pallas_call(functools.partial(fused_kernel, nd, nv), in_specs=[hbm] *...]
where the time goes in v3:
time: 67.8 us; the launch traced here: 67.6 us
  Pallas kernels  64.2 us (95%)
  local copies, waits for them, and re-layouts  2.74 us (4%)
    pallas_call x1, Pallas kernels, per_device(): pl.pallas_call(functools.partial(fused_kernel, nd, nv), in_specs=[hbm] *...  64.2 us
    slice x2, local copies, waits for them, and re-layouts, per_device(): return (out[:, depth], out[:, :depth].astype(bf16))  2.74 us

profile of v3, /device:TPU:0, one launch (start us, length us, event | category | flops | bytes accessed | tf_op | source)
XLA Modules:
  0.0 67.6 jit_solution(15076953916008128543)
XLA Ops:
  0.6 64.2 %fused_head.1 = f32[4,3712]{1,0:T(4,128)} custom-call(bf16[4,3584]{1,0:T(4,128)(2,1)} %hid_hbm.1, s32[4,128]{1,0:T(4,128)} %ids_hbm.1, f32[4,128]{1,0:T(4,128)} %probs_hbm.1, s32[4]{0:T(128)} %targets_hbm.1, bf16[8000,3584]{1,0:T(8,128)(2,1)} %bitcast.1), custom_call_target="tpu_custom_call" | custom-call | flops 14680064000 | bytes 57344000 | tf_op jit(solution)/shard_map/fused_head/pallas_call | solution.py:464
  64.9 1.3 %slice_reduce_fusion = f32[4]{0:T(128)} fusion(f32[4,3712]{1,0:T(4,128)} %fused_head.1), kind=kLoop, calls=%fused_computation.1 | loop fusion | bytes 32 | tf_op jit(solution)/shard_map/slice | solution.py:505
  66.2 1.4 %slice.12 = bf16[4,3584]{1,0:T(4,128)(2,1)} slice(f32[4,3712]{1,0:T(4,128)} %fused_head.1), slice={[0:4], [0:3584]} | slice | bytes 57344 | tf_op jit(solution)/shard_map/slice | solution.py:505

commit v4 on v3

--- a/solution.py
+++ b/solution.py
@@ -445,6 +445,13 @@
         pltpu.VMEM((rows, depth), jnp.float32),
         pltpu.VMEM((half, depth), jnp.bfloat16),
         pltpu.VMEM((nz, local_tokens, depth), jnp.bfloat16))
+
+
+def split_kernel(both_ref, loss_ref, grad_ref):
+    local_tokens, depth = grad_ref.shape
+    grad_ref[...] = both_ref[:, :depth].astype(jnp.bfloat16)
+    for i in range(local_tokens):
+        loss_ref[i] = jnp.max(both_ref[i:i + 1, depth:])
 
 
 def per_device(nd, nv, hidden, head_weight, teacher_ids, teacher_probs, target_ids):
@@ -502,7 +509,15 @@
             transcendentals=2 * tokens * width),
         name="fused_head",
     )(hidden, teacher_ids, teacher_probs, target_ids, head_weight.T)
-    return out[:, depth], out[:, :depth].astype(bf16)
+    return tuple(pl.pallas_call(
+        split_kernel,
+        in_specs=[pl.BlockSpec(memory_space=pltpu.VMEM)],
+        out_specs=[pl.BlockSpec(memory_space=pltpu.SMEM),
+                   pl.BlockSpec(memory_space=pltpu.VMEM)],
+        out_shape=[jax.ShapeDtypeStruct((local_tokens,), f32),
+                   jax.ShapeDtypeStruct((local_tokens, depth), bf16)],
+        name="split_outputs",
+    )(out))
 
 
 def solution(mesh):

time: 67.8 us -> 66.7 us (0.984)
  local copies, waits for them, and re-layouts: 2.74 us -> 0 us
  Pallas kernels: 64.2 us -> 65.7 us
    slice x2 -> x0, local copies, waits for them, and re-layouts: 2.74 us -> none  [per_device(): return (out[:, depth], out[:, :depth].astype(bf16))]
    pallas_call x0 -> x1, Pallas kernels: none -> 1.46 us  [per_device(): pl.pallas_call(split_kernel, in_specs=[pl.BlockSpec(memory_space=pltpu.VM...]
where the time goes in v4:
time: 66.7 us; the launch traced here: 66.5 us
  Pallas kernels  65.7 us (99%)
  between operations  0.8 us (1%)
    pallas_call x1, Pallas kernels, per_device(): pl.pallas_call(functools.partial(fused_kernel, nd, nv), in_specs=[hbm] *...  64.2 us
    pallas_call x1, Pallas kernels, per_device(): pl.pallas_call(split_kernel, in_specs=[pl.BlockSpec(memory_space=pltpu.VM...  1.46 us

profile of v4, /device:TPU:0, one launch (start us, length us, event | category | flops | bytes accessed | tf_op | source)
XLA Modules:
  0.0 66.5 jit_solution(16220034699715713487)
XLA Ops:
  0.6 64.2 %fused_head.1.both_ref = f32[4,3712]{1,0:T(4,128)} custom-call(bf16[4,3584]{1,0:T(4,128)(2,1)} %hid_hbm.1, s32[4,128]{1,0:T(4,128)} %ids_hbm.1, f32[4,128]{1,0:T(4,128)} %probs_hbm.1, s32[4]{0:T(128)} %targets_hbm.1, bf16[8000,3584]{1,0:T(8,128)(2,1)} %bitcast.1), custom_call_target="tpu_custom_call" | custom-call | flops 14680064000 | bytes 57344000 | tf_op jit(solution)/shard_map/fused_head/pallas_call | solution.py:471
  64.9 1.5 %split_outputs.1 = (f32[4]{0:T(128)}, bf16[4,3584]{1,0:T(4,128)(2,1)}) custom-call(f32[4,3712]{1,0:T(4,128)} %fused_head.1.both_ref), custom_call_target="tpu_custom_call" | custom-call | tf_op jit(solution)/shard_map/split_outputs/pallas_call | solution.py:512

commit v5 on v4

--- a/solution.py
+++ b/solution.py
@@ -13,7 +13,7 @@
 CHUNK = 768
 LANES = 128
 PIECES = 2
-LAG = 2
+LAG = 3
 AXES = ("dp", "vocab")
 MESH = pl.DeviceIdType.MESH
 NT = (((1,), (1,)), ((), ()))

time: 66.7 us -> 66.6 us (level)
  no operation moved by 1% of the time
where the time goes in v5:
time: 66.6 us; the launch traced here: 66.4 us
  Pallas kernels  65.6 us (98%)
  between operations  0.8 us (1%)
    pallas_call x1, Pallas kernels, per_device(): pl.pallas_call(functools.partial(fused_kernel, nd, nv), in_specs=[hbm] *...  64.2 us
    pallas_call x1, Pallas kernels, per_device(): pl.pallas_call(split_kernel, in_specs=[pl.BlockSpec(memory_space=pltpu.VM...  1.46 us

profile of v5, /device:TPU:0, one launch (start us, length us, event | category | flops | bytes accessed | tf_op | source)
XLA Modules:
  0.0 66.4 jit_solution(696131113822417231)
XLA Ops:
  0.6 64.2 %fused_head.1.both_ref = f32[4,3712]{1,0:T(4,128)} custom-call(bf16[4,3584]{1,0:T(4,128)(2,1)} %hid_hbm.1, s32[4,128]{1,0:T(4,128)} %ids_hbm.1, f32[4,128]{1,0:T(4,128)} %probs_hbm.1, s32[4]{0:T(128)} %targets_hbm.1, bf16[8000,3584]{1,0:T(8,128)(2,1)} %bitcast.1), custom_call_target="tpu_custom_call" | custom-call | flops 14680064000 | bytes 57344000 | tf_op jit(solution)/shard_map/fused_head/pallas_call | solution.py:471
  64.8 1.5 %split_outputs.1 = (f32[4]{0:T(128)}, bf16[4,3584]{1,0:T(4,128)(2,1)}) custom-call(f32[4,3712]{1,0:T(4,128)} %fused_head.1.both_ref), custom_call_target="tpu_custom_call" | custom-call | tf_op jit(solution)/shard_map/split_outputs/pallas_call | solution.py:512
